TPU v7x, 256 devices: a whole 4x4x8 slice. The times are simulated.
256 devices in a mesh: dp: 16 (over z_hi, x), ctx: 16 (over z_lo, y, core).
Axes of the slice: x: 4, y: 4, z: 8 (z_hi: 4, z_lo: 2; z = z_hi * 2 + z_lo), core: 2. Of those that a mesh axis runs over, the one named last changes fastest.
Arguments:
- queries: bfloat16 [16, 2, 16, 64, 2048], P('dp', None, 'ctx'), may hold values from -24 to 24
- key_states: bfloat16 [16, 2, 16, 64, 512], P('dp', None, 'ctx'), may hold values from -24 to 24
- value_vectors: bfloat16 [16, 2, 16, 64, 512], P('dp', None, 'ctx'), may hold values from -6 to 6
- grad_out: bfloat16 [16, 2, 16, 64, 2048], P('dp', None, 'ctx'), may hold values from -6 to 6
- doc_start: int32 [16, 2, 16, 64], P('dp', None, 'ctx'), may hold values from 0 to 32767, as said below
Outputs:
- attn_out: bfloat16 [16, 2, 16, 64, 2048], P('dp', None, 'ctx')
- q_grad: bfloat16 [16, 2, 16, 64, 2048], P('dp', None, 'ctx')
- k_grad: bfloat16 [16, 2, 16, 64, 512], P('dp', None, 'ctx')
- v_grad: bfloat16 [16, 2, 16, 64, 512], P('dp', None, 'ctx')
Inputs may be any that keep to these rules, and one draw needn't show every extreme that they name: Every token from doc_start of a token to that token's own position belongs to its document and carries the same doc_start; documents have at most 2048 tokens and one has exactly 2048; every document except the sequence's last token, which is a document of its own, has at least 512 tokens; a document that reaches into the positions of cycle d from an earlier cycle begins at or after position d * 2048 - 2048 // 2.
All inputs are finite; a program needn't handle non-finite values.
Results may differ from a plain program's by a relative error of at most 0.027.
Values may be sent and summed in bfloat16 or wider, within the bound.
No kernel may reach another device: no remote copies, remote signals or barrier semaphores. Data moves between devices by JAX's collectives and lax.ppermute only.
A program may use at most 128 MiB of HBM per device.

v0:
```python
from functools import partial

import jax
import jax.numpy as jnp
from jax import lax
from jax.experimental import pallas as pl
from jax.experimental.pallas import tpu as pltpu
from jax.sharding import PartitionSpec as P

HEAD = 128
HALF = 64
MEMBERS = 16
HEADS = 16
GROUPS = 4
SPAN = 2048
BACK = 1024
TQ = 512
TK = 512
QB = SPAN // TQ
QS = TQ // HALF
KS = TK // HALF
OWN_TILES = SPAN // TK
BACK_TILES = BACK // TK
SCALE = HEAD**-0.5
FOLD = SCALE * 1.4426950408889634
NEG = -1e30
BF = jnp.bfloat16
F32 = jnp.float32

IN_Q, IN_G, IN_X, IN_S, IN_ROWS = 0, 128, 256, 448, 464
OUT_A, OUT_Q, OUT_X, OUT_ROWS = 0, 128, 256, 384

NT = (((1,), (1,)), ((), ()))
NN = (((1,), (0,)), ((), ()))


def dot(a, b, dims=NN):
    return lax.dot_general(a, b, dims, preferred_element_type=F32)


def begin(pairs, sems):
    copies = [pltpu.make_async_copy(a, b, sems.at[i]) for i, (a, b) in enumerate(pairs)]
    for c in copies:
        c.start()
    return copies


def finish(copies):
    for c in copies:
        c.wait()


def columns(n):
    return pl.ds(n * HEAD, HEAD)


def pack_kernel(q_ref, g_ref, k_ref, v_ref, o_ref, sems):
    pairs = []
    for n in range(HEADS):
        x_ref = k_ref if n % 2 == 0 else v_ref
        pairs.append((q_ref.at[:, columns(n)], o_ref.at[n, pl.ds(IN_Q, 128)]))
        pairs.append((g_ref.at[:, columns(n)], o_ref.at[n, pl.ds(IN_G, 128)]))
        pairs.append((x_ref.at[:, columns(n // 4)], o_ref.at[n, pl.ds(IN_X, 128)]))
    finish(begin(pairs, sems))


def pack_tail_kernel(tail_ref, s_ref, old_ref, o_ref, x_s, sems):
    del old_ref
    for n in range(HEADS):
        row = (n % 2) * HALF
        x_s[n, 0:HALF] = tail_ref[row : row + HALF, n // 4 * HEAD : (n // 4 + 1) * HEAD]
        x_s[n, HALF : HALF + 16] = s_ref[...]
    finish(begin([(x_s, o_ref.at[:, pl.ds(IN_X + 128, HALF + 16)])], sems))


def low_position(i):
    source = (i - QB // 2) * QS + QS - 1
    upper = (2 * MEMBERS - 1 - source) * HALF
    return BACK + jnp.where(i >= QB // 2, upper, i * TQ)


def block_of(i, st_ref, plan_ref):
    lane = lax.broadcasted_iota(jnp.int32, (1, TQ), 1)
    part = lane // HALF
    part = jnp.where(i >= QB // 2, QS - 1 - part, part)
    low = low_position(i)
    end = (low + TQ - 1) // TK + 1
    whole = (plan_ref[2 * QB + i], low)
    return st_ref[i], low + part * HALF + lane % HALF, plan_ref[QB + i], end, whole


def masked(s, start, last, base, turned, fill=NEG):
    rows = lax.broadcasted_iota(jnp.int32, (HALF, TQ), 0)
    parts = []
    for b in range(KS):
        off = base + HALF * jnp.where(turned, KS - 1 - b, b)
        seen = (rows >= start - off) & (rows <= last - off)
        parts.append(jnp.where(seen, s[b * HALF : (b + 1) * HALF], fill))
    return jnp.concatenate(parts, axis=0)


def place(t):
    upper = t >= BACK_TILES + OWN_TILES // 2
    turned = (t < BACK_TILES) | upper
    top = jnp.where(upper, 2 * BACK_TILES + OWN_TILES + OWN_TILES // 2 - 1, BACK_TILES - 1)
    return jnp.where(turned, top - t, t), turned


def packet_rows(ref, i, row):
    half = pl.ds(pl.multiple_of(row + (i // 2) * HALF, HALF), HALF)
    return ref[pl.ds((i % 2) * QS, QS), half].reshape(TQ, HEAD)


def rows_of(ref, at, count):
    return ref[pl.ds(at * count, count)].reshape(count * HALF, HEAD)


def inside(whole, t):
    return (t * TK >= whole[0]) & (t * TK + TK - 1 <= whole[1])


def softmax_tiles(lo, hi, qi, start, last, clear, kv_s, vt_s, acc_s, p_s, m_s):
    acc_s[...] = jnp.zeros_like(acc_s)

    def tile(whole, t, m, l8):
        at, turned = place(t)
        s = dot(rows_of(kv_s.at[0], at, KS), qi, NT) * FOLD
        if not whole:
            s = masked(s, start, last, t * TK, turned)
        m_new = jnp.maximum(m, jnp.max(s, axis=0, keepdims=True))
        p = jnp.exp2(s - m_new)
        p_s[t] = p
        m_s[t] = m_new
        keep = jnp.exp2(m - m_new)
        l8 = l8 * keep + jnp.sum(p.reshape(TK // 8, 8, TQ), axis=0)
        acc_s[...] = acc_s[...] * keep + dot(vt_s[at], p.astype(BF))
        return m_new, l8

    def either(t, carry):
        return lax.cond(
            inside(clear, t), partial(tile, True), partial(tile, False), t, *carry
        )

    return lax.fori_loop(
        lo, hi, either, (jnp.full((1, TQ), NEG, F32), jnp.zeros((8, TQ), F32))
    )


def grad_tile(p, at, base, qi, gi, delta, kv_s, kt_s, dk_s, dv_s, dq_s):
    dp = dot(rows_of(kv_s.at[1], at, KS), gi, NT)
    at = at - base
    ds = (p * (dp - delta)).astype(BF)
    dv_s[at] += dot(p.astype(BF), gi)
    dk_s[at] += dot(ds, qi)
    dq_s[...] += dot(kt_s[at], ds)


def grad_tiles(lo, hi, base, qi, gi, start, last, clear, lse, delta, kv_s, kt_s, dk_s, dv_s, dq_s):
    def tile(whole, t):
        at, turned = place(t)
        s = dot(rows_of(kv_s.at[0], at, KS), qi, NT) * FOLD - lse
        if not whole:
            s = masked(s, start, last, t * TK, turned)
        grad_tile(jnp.exp2(s), at, base, qi, gi, delta, kv_s, kt_s, dk_s, dv_s, dq_s)
        return 0

    def either(t, _):
        return lax.cond(inside(clear, t), partial(tile, True), partial(tile, False), t)

    lax.fori_loop(lo, hi, either, 0)


def kept_tiles(lo, hi, base, qi, gi, lse, delta, kv_s, kt_s, dk_s, dv_s, dq_s, p_s, m_s):
    def tile(t, _):
        p = p_s[t] * jnp.exp2(m_s[t] - lse)
        grad_tile(p, place(t)[0], base, qi, gi, delta, kv_s, kt_s, dk_s, dv_s, dq_s)
        return 0

    lax.fori_loop(lo, hi, tile, 0)


def forward_block(i, qi, gi, start, last, clear, first, end, kv_s, vt_s, acc_s, p_s, m_s, out_ref):
    m, l8 = softmax_tiles(first, end, qi, start, last, clear, kv_s, vt_s, acc_s, p_s, m_s)
    l = jnp.sum(l8, axis=0, keepdims=True)
    out_t = acc_s[...] * (1.0 / l)
    delta = jnp.sum(out_t * gi.astype(F32).T, axis=0, keepdims=True)
    store_block(i, OUT_A, out_t.T.astype(BF), out_ref)
    return m + jnp.log2(l), delta


def store_block(i, row, value, out_ref):
    half = pl.ds(pl.multiple_of(row + (i // 2) * HALF, HALF), HALF)
    out_ref[pl.ds((i % 2) * QS, QS), half] = value.reshape(QS, HALF, HEAD)


def block_out(i, row, o_s, out_ref, sem):
    at = (
        pl.ds((i % 2) * QS, QS),
        pl.ds(pl.multiple_of(row + (i // 2) * HALF, HALF), HALF),
    )
    return pltpu.make_async_copy(o_s.at[at], out_ref.at[at], sem)


def forward_kernel(
    core_ref, a_ref, x_ref,
    st_ref, kv_s, lse_ref, delta_ref, out_ref, dq_ref, keep_ref, give_ref, plan_ref,
    vt_s, kt_s, acc_s, p_s, m_s, dk_s, dv_s, sems,
):
    del sems
    core = core_ref[0]
    for part, row in enumerate((128, 0, HALF)):
        at = slice(part * MEMBERS, (part + 1) * MEMBERS)
        mine = a_ref[:, IN_X + row : IN_X + row + HALF]
        theirs = x_ref[:, row : row + HALF]
        kv_s[0, at] = jnp.where(core == 0, mine, theirs)
        kv_s[1, at] = jnp.where(core == 0, theirs, mine)
    for t in range(SPAN // 128):
        s0, row = (2 * t, 0) if t < 8 else (2 * t - 16, 2)
        both = a_ref[s0, IN_S : IN_S + 16].astype(F32) + a_ref[s0 + 1, IN_S : IN_S + 16].astype(F32)
        start = both[row : row + 1] * 64.0 + both[row + 1 : row + 2]
        c = (t % 4) * 128
        st_ref[t // 4, 0:1, c : c + 128] = start.astype(jnp.int32)
    for t in range(BACK_TILES + OWN_TILES):
        vt_s[t] = rows_of(kv_s.at[1], t, KS).T
    for t in range(BACK_TILES):
        kt_s[t] = rows_of(kv_s.at[0], t, KS).T
    dk_s[...] = jnp.zeros_like(dk_s)
    dv_s[...] = jnp.zeros_like(dv_s)

    spans = []
    for i in range(QB):
        first = jnp.min(st_ref[i]) // TK
        plan_ref[QB + i] = first
        plan_ref[2 * QB + i] = jnp.max(st_ref[i])
        spans.append((first, (low_position(i) + TQ - 1) // TK + 1))
    budget = core_ref[1]
    for first, end in spans:
        reach = jnp.maximum(BACK_TILES - first, 0)
        budget -= jnp.where(reach > 0, 4 * (end - first) + 5 * reach + 2, 0)
    for i, (first, end) in enumerate(spans):
        need = 4 * (end - first) + 2
        extra = (first >= BACK_TILES) & (need <= budget)
        budget -= jnp.where(extra, need, 0)
        plan_ref[i] = ((first < BACK_TILES) | extra).astype(jnp.int32)

    def q_block(i, _):
        @pl.when(plan_ref[i] == 1)
        def _():
            start, last, first, end, clear = block_of(i, st_ref, plan_ref)
            qi = packet_rows(a_ref, i, IN_Q)
            gi = packet_rows(a_ref, i, IN_G)
            lse, delta = forward_block(
                i, qi, gi, start, last, clear, first, end, kv_s, vt_s, acc_s, p_s, m_s, out_ref
            )
            lse_ref[i] = lse
            delta_ref[i] = delta
            dq_ref[i] = jnp.zeros((HEAD, TQ), F32)
            kept_tiles(
                first,
                BACK_TILES,
                0,
                qi,
                gi,
                lse,
                delta,
                kv_s,
                kt_s,
                dk_s,
                dv_s,
                dq_ref.at[i],
                p_s,
                m_s,
            )

        return 0

    lax.fori_loop(0, QB, q_block, 0)
    even = core == 0
    for t in range(BACK_TILES):
        dk, dv = dk_s[t] * SCALE, dv_s[t]
        at = slice(t * KS, (t + 1) * KS)
        keep_ref[at] = jnp.where(even, dk, dv).astype(BF).reshape(KS, HALF, HEAD)
        give_ref[at] = jnp.where(even, dv, dk).astype(BF).reshape(KS, HALF, HEAD)


def own_kernel(
    core_ref, plan_ref, a_ref, kv_ref, st_ref, lse_ref, delta_ref, dq_ref, old_ref, after_ref,
    out_ref, keep_ref, give_ref,
    vt_s, kt_s, acc_s, p_s, m_s, dq_s, o_s, dk_s, dv_s, sems,
):
    del old_ref, after_ref
    core = core_ref[0]
    dk_s[...] = jnp.zeros_like(dk_s)
    dv_s[...] = jnp.zeros_like(dv_s)
    for t in range(OWN_TILES):
        kt_s[t] = rows_of(kv_ref.at[0], BACK_TILES + t, KS).T
        vt_s[BACK_TILES + t] = rows_of(kv_ref.at[1], BACK_TILES + t, KS).T

    def q_block(i, _):
        qi = packet_rows(a_ref, i, IN_Q)
        gi = packet_rows(a_ref, i, IN_G)
        start, last, first, end, clear = block_of(i, st_ref, plan_ref)

        low = jnp.maximum(first, BACK_TILES)

        @pl.when(plan_ref[i] == 0)
        def _():
            lse, delta = forward_block(
                i, qi, gi, start, last, clear, first, end, kv_ref, vt_s, acc_s, p_s, m_s, o_s
            )
            dq_s[...] = jnp.zeros_like(dq_s)
            kept_tiles(
                low,
                end,
                BACK_TILES,
                qi,
                gi,
                lse,
                delta,
                kv_ref,
                kt_s,
                dk_s,
                dv_s,
                dq_s,
                p_s,
                m_s,
            )

        @pl.when(plan_ref[i] == 1)
        def _():
            dq_s[...] = dq_ref[i]
            grad_tiles(
                low,
                end,
                BACK_TILES,
                qi,
                gi,
                start,
                last,
                clear,
                lse_ref[i],
                delta_ref[i],
                kv_ref,
                kt_s,
                dk_s,
                dv_s,
                dq_s,
            )

        store_block(i, OUT_Q, (dq_s[...] * SCALE).T.astype(BF), o_s)
        block_out(i, OUT_Q, o_s, out_ref, sems.at[i]).start()

        @pl.when(plan_ref[i] == 0)
        def _():
            copy = block_out(i, OUT_A, o_s, out_ref, sems.at[QB])
            copy.start()
            copy.wait()

        return 0

    lax.fori_loop(0, QB, q_block, 0)
    for i in range(QB):
        block_out(i, OUT_Q, o_s, out_ref, sems.at[i]).wait()
    even = core == 0
    for t in range(OWN_TILES):
        dk, dv = dk_s[t] * SCALE, dv_s[t]
        half, s0 = t // (OWN_TILES // 2), (t % (OWN_TILES // 2)) * KS
        at = (slice(s0, s0 + KS), slice(half * HALF, half * HALF + HALF))
        keep_ref[at] = jnp.where(even, dk, dv).astype(BF).reshape(KS, HALF, HEAD)
        give_ref[at] = jnp.where(even, dv, dk).astype(BF).reshape(KS, HALF, HEAD)


def tie_kernel(x_ref, after_ref, o_ref, sems):
    del x_ref, after_ref, o_ref, sems


def merge_kernel(keep_ref, got_ref, back_ref, old_ref, out_ref, x_s, sems):
    lower, upper = slice(0, HALF), slice(HALF, 2 * HALF)
    x_s[:, lower] = (keep_ref[:, lower].astype(F32) + got_ref[:, lower].astype(F32)).astype(BF)
    total = keep_ref[:, upper].astype(F32) + got_ref[:, upper].astype(F32)
    x_s[:, upper] = (total + back_ref[...].astype(F32)).astype(BF)
    finish(begin([(x_s, out_ref.at[:, pl.ds(OUT_X, 128)])], sems))


def unpack_kernel(t_ref, a_ref, q_ref, k_ref, v_ref, sems):
    pairs = []
    for n in range(HEADS):
        pairs.append((t_ref.at[n, pl.ds(OUT_A, 128)], a_ref.at[:, columns(n)]))
        pairs.append((t_ref.at[n, pl.ds(OUT_Q, 128)], q_ref.at[:, columns(n)]))
    copies = begin(pairs, sems)
    for g in range(GROUPS):
        at = slice(g * HEAD, (g + 1) * HEAD)
        for n, o_ref in ((4 * g, k_ref), (4 * g + 1, v_ref)):
            total = t_ref[n, OUT_X : OUT_X + 128].astype(F32) + t_ref[
                n + 2, OUT_X : OUT_X + 128
            ].astype(F32)
            o_ref[:, at] = total.astype(BF)
    finish(copies)


def shape(dims, dtype=BF):
    return jax.ShapeDtypeStruct(dims, dtype)


HBM = pl.BlockSpec(memory_space=pltpu.HBM)
VMEM = pl.BlockSpec(memory_space=pltpu.VMEM)
SMEM = pl.BlockSpec(memory_space=pltpu.SMEM)


def call(kernel, name, us, ins, outs, scratch, copies, mib=32, **more):
    return pl.pallas_call(
        kernel,
        in_specs=ins,
        out_specs=[space for space, _ in outs],
        out_shape=[what for _, what in outs],
        scratch_shapes=scratch + [pltpu.SemaphoreType.DMA((copies,))],
        compiler_params=pltpu.CompilerParams(vmem_limit_bytes=mib * 1024 * 1024),
        cost_estimate=pl.CostEstimate(
            flops=int(us * 4e8), bytes_accessed=1 << 20, transcendentals=0
        ),
        name=name,
        **more,
    )


def tie(x, after):
    (x,) = call(
        tie_kernel,
        "tie",
        1,
        [HBM, HBM],
        [(HBM, shape(x.shape))],
        [],
        1,
        input_output_aliases={0: 0},
    )(x, after)
    return x


def on_device(queries, key_states, value_vectors, grad_out, doc_start):
    cycle = lax.axis_index("dp")
    core = lax.axis_index("ctx") % 2
    q = queries.reshape(128, HEADS * HEAD)
    g = grad_out.reshape(128, HEADS * HEAD)
    k = key_states.reshape(128, GROUPS * HEAD)
    v = value_vectors.reshape(128, GROUPS * HEAD)
    swap = [(i, i ^ 1) for i in range(MEMBERS)]
    budget = jnp.where(cycle % 4 == 0, 0, jnp.where(cycle % 4 == 1, 64, 40))
    which = jnp.stack([core, budget])

    rel = doc_start.reshape(2, HALF) - (cycle * SPAN - BACK)
    parts = jnp.stack([rel // 64, rel % 64], axis=1).reshape(4, HALF).astype(BF)
    zero = jnp.zeros_like(parts)
    starts = jnp.where(
        core == 0,
        jnp.concatenate([parts, zero], axis=1),
        jnp.concatenate([zero, parts], axis=1),
    )
    starts = jnp.pad(starts, ((0, 12), (0, 0)))

    wide = (VMEM, shape((QB, HEAD, TQ), F32))
    line = (VMEM, shape((QB, 1, TQ), F32))

    def turned(tiles):
        return pltpu.VMEM((tiles, HEAD, TK), BF)

    def sums(tiles):
        return pltpu.VMEM((tiles, TK, HEAD), F32)

    tail = jnp.concatenate([k[HALF:], v[HALF:]], axis=0)
    tail = lax.ppermute(tail, "dp", [(i, i + 1) for i in range(15)])
    kept = [
        pltpu.VMEM((BACK_TILES + OWN_TILES, TK, TQ), F32),
        pltpu.VMEM((BACK_TILES + OWN_TILES, 1, TQ), F32),
    ]
    packets = shape((HEADS, IN_ROWS, HEAD))
    (a,) = call(
        pack_kernel,
        "pack",
        1,
        [HBM, HBM, HBM, HBM],
        [(VMEM, packets)],
        [],
        3 * HEADS,
    )(*(pltpu.with_memory_space_constraint(each, pltpu.HBM) for each in (q, g, k, v)))
    (a,) = call(
        pack_tail_kernel,
        "pack_tail",
        1,
        [VMEM, VMEM, pl.BlockSpec(memory_space=pl.ANY)],
        [(pl.BlockSpec(memory_space=pl.ANY), packets)],
        [pltpu.VMEM((HEADS, HALF + 16, HEAD), BF)],
        1,
        input_output_aliases={2: 0},
    )(tail, starts, a)
    a = lax.all_to_all(a, "ctx", 0, 0, tiled=True)
    x = lax.ppermute(a[:, IN_X : IN_X + 192], "ctx", swap)
    st, kv, lse, delta, out, dq, keep_back, give_back, plan = call(
        forward_kernel,
        "forward",
        16,
        [SMEM, VMEM, VMEM],
        [
            (VMEM, shape((QB, 1, TQ), jnp.int32)),
            (VMEM, shape((2, 3 * MEMBERS, HALF, HEAD))),
            line,
            line,
            (VMEM, shape((MEMBERS, OUT_ROWS, HEAD))),
            wide,
            (VMEM, shape((MEMBERS, HALF, HEAD))),
            (VMEM, shape((MEMBERS, HALF, HEAD))),
            (SMEM, shape((3 * QB,), jnp.int32)),
        ],
        [turned(BACK_TILES + OWN_TILES), turned(BACK_TILES), pltpu.VMEM((HEAD, TQ), F32)]
        + kept
        + [sums(BACK_TILES), sums(BACK_TILES)],
        1,
    )(which, a, x)
    got_back = lax.ppermute(give_back, "ctx", swap)
    back = (keep_back.astype(F32) + got_back.astype(F32)).astype(BF)
    sent_back = lax.ppermute(back, "dp", [(i + 1, i) for i in range(15)])
    out, keep, give = call(
        own_kernel,
        "own",
        11,
        [SMEM, SMEM, VMEM, VMEM, VMEM, VMEM, VMEM, VMEM, HBM, HBM],
        [
            (HBM, shape((MEMBERS, OUT_ROWS, HEAD))),
            (VMEM, shape((MEMBERS, 128, HEAD))),
            (VMEM, shape((MEMBERS, 128, HEAD))),
        ],
        [
            turned(BACK_TILES + OWN_TILES),
            turned(OWN_TILES),
            pltpu.VMEM((HEAD, TQ), F32),
            *kept,
            pltpu.VMEM((HEAD, TQ), F32),
            pltpu.VMEM((MEMBERS, OUT_X, HEAD), BF),
            sums(OWN_TILES),
            sums(OWN_TILES),
        ],
        QB + 1,
        input_output_aliases={8: 0},
    )(which, plan, a, kv, st, lse, delta, dq, out, back)
    got = lax.ppermute(tie(give, sent_back), "ctx", swap)
    (out,) = call(
        merge_kernel,
        "merge",
        1,
        [VMEM, VMEM, VMEM, HBM],
        [(HBM, shape((MEMBERS, OUT_ROWS, HEAD)))],
        [pltpu.VMEM((MEMBERS, 128, HEAD), BF)],
        1,
        input_output_aliases={3: 0},
    )(keep, got, sent_back, out)
    out = lax.all_to_all(out, "ctx", 0, 0, tiled=True)
    attn, q_grad, k_grad, v_grad = call(
        unpack_kernel,
        "unpack",
        2,
        [VMEM],
        [(HBM, shape(q.shape)), (HBM, shape(q.shape)), (VMEM, shape(k.shape)), (VMEM, shape(k.shape))],
        [],
        2 * HEADS,
    )(out)
    return (
        attn.reshape(queries.shape),
        q_grad.reshape(queries.shape),
        k_grad.reshape(key_states.shape),
        v_grad.reshape(value_vectors.shape),
    )


def solution(mesh):
    wide = P("dp", None, "ctx", None, None)
    return jax.shard_map(
        on_device,
        mesh=mesh,
        in_specs=(wide, wide, wide, wide, P("dp", None, "ctx", None)),
        out_specs=(wide, wide, wide, wide),
        check_vma=False,
    )
```

profile of v0, /device:TPU:6, one launch (start us, length us, event | category | flops | bytes accessed | tf_op | source)
XLA Modules:
  0.0 105.7 jit_solution(8569898169540096884)
XLA Ops:
  0.6 0.9 slice_bitcast_fusion
  1.5 5.1 %collective-permute-start = (bf16[128,512]{1,0:T(8,128)(2,1)S(1)}, bf16[128,512]{1,0:T(8,128)(2,1)S(1)}, u32[]{:S(2)}, u32[]{:S(2)}) collective-permute-start(bf16[128,512]{1,0:T(8,128)(2,1)S(1)} %pad_maximum_fusion), channel_id=1, source_target_pairs={{0,16},{16,32},{32,48},{48,64},{64,80},{80,96},{96,112},{112,128},... | collective-permute-start | bytes 393224 | tf_op jit(solution)/shard_map/ppermute | solution.py:471
  6.7 0.7 broadcast_subtract_fusion
  7.4 0.1 pad_select_fusion
  7.5 1.8 %pack.1.old_ref = bf16[16,464,128]{2,1,0:T(8,128)(2,1)S(1)} custom-call(bf16[128,2048]{1,0:T(8,128)(2,1)} %bitcast.24, bf16[128,2048]{1,0:T(8,128)(2,1)} %bitcast.25, bf16[128,512]{1,0:T(8,128)(2,1)} %bitcast.27, bf16[128,512]{1,0:T(8,128)(2,1)} %bitcast.26), custom_call_target="tpu_custom_call" | custom-call | flops 400000000 | bytes 1048576 | tf_op jit(solution)/shard_map/pack/pallas_call | solution.py:477
  9.3 0.2 collective-permute-done.tail_ref
  9.4 0.1 pack_tail.1
  9.5 33.7 %all_to_all.10.a_ref = bf16[16,464,128]{2,1,0:T(8,128)(2,1)S(1)} all-to-all(bf16[16,464,128]{2,1,0:T(8,128)(2,1)S(1)} %pack_tail.1), channel_id=1, replica_groups=mesh['dp'=16,'ctx'=16] {'ctx'}, dimensions={0} | all-to-all | bytes 3801088 | tf_op jit(solution)/shard_map/all_to_all | solution.py:496
  43.2 0.1 slice.20
  43.3 0.1 collective-permute-start.1
  43.4 0.1 pad_add_fusion.core_ref
  43.5 2.2 %collective-permute-done.1.x_ref = bf16[16,192,128]{2,1,0:T(8,128)(2,1)S(1)} collective-permute-done((bf16[16,192,128]{2,1,0:T(8,128)(2,1)S(1)}, bf16[16,192,128]{2,1,0:T(8,128)(2,1)S(1)}, u32[]{:S(2)}, u32[]{:S(2)}) %collective-permute-start.1) | collective-permute-done | bytes 786464 | tf_op jit(solution)/shard_map/ppermute | solution.py:497
  45.6 10.5 %forward.1 = (s32[4,1,512]{2,1,0:T(1,128)S(1)}, bf16[2,48,64,128]{3,2,1,0:T(8,128)(2,1)S(1)}, f32[4,1,512]{2,1,0:T(1,128)S(1)}, f32[4,1,512]{2,1,0:T(1,128)S(1)}...) custom-call(s32[2]{0:T(128)S(1)} %pad_add_fusion.core_ref, ...), custom_call_target="tpu_custom_call" | custom-call | flops 6400000000 | bytes 1048576 | tf_op jit(solution)/shard_map/forward/pallas_call | solution.py:498
  56.1 0.2 collective-permute-start.2
  56.3 1.4 %collective-permute-done.2 = bf16[16,64,128]{2,1,0:T(8,128)(2,1)S(1)} collective-permute-done((bf16[16,64,128]{2,1,0:T(8,128)(2,1)S(1)}, bf16[16,64,128]{2,1,0:T(8,128)(2,1)S(1)}, u32[]{:S(2)}, u32[]{:S(2)}) %collective-permute-start.2) | collective-permute-done | bytes 262176 | tf_op jit(solution)/shard_map/ppermute | solution.py:519
  57.8 0.1 add_convert_fusion.after_ref
  57.8 1.9 %collective-permute-start.3 = (bf16[16,64,128]{2,1,0:T(8,128)(2,1)S(1)}, bf16[16,64,128]{2,1,0:T(8,128)(2,1)S(1)}, u32[]{:S(2)}, u32[]{:S(2)}) collective-permute-start(bf16[16,64,128]{2,1,0:T(8,128)(2,1)S(1)} %add_convert_fusion.after_ref), channel_id=1, source_target_pairs={{16,0},{32,16},{48,32},{64,48},{80,64},{96,80},{112,96},{128,112},... | collective-permute-start | bytes 786440 | tf_op jit(solution)/shard_map/ppermute | solution.py:521
  59.8 11.4 %own.1 = (bf16[16,384,128]{2,1,0:T(8,128)(2,1)S(1)}, bf16[16,128,128]{2,1,0:T(8,128)(2,1)S(1)}, bf16[16,128,128]{2,1,0:T(8,128)(2,1)S(1)}) custom-call(s32[2]{0:T(128)S(1)} %pad_add_fusion.core_ref, s32[12]{0:T(128)S(1)} %get-tuple-element.20.plan_ref, bf16[16,464,128]{2,1,0:T(8,128)(2,1)S(1)} %all_to_all.10.a_ref, ...), custom_call_target="tpu_custom_call", output_to_operand_aliasing={{0}: (8, {})} | custom-call | flops 4400000000 | bytes 1048576 | tf_op jit(solution)/shard_map/own/pallas_call | solution.py:522
  71.2 5.6 %collective-permute-done.3.after_ref.back_ref = bf16[16,64,128]{2,1,0:T(8,128)(2,1)S(1)} collective-permute-done((bf16[16,64,128]{2,1,0:T(8,128)(2,1)S(1)}, bf16[16,64,128]{2,1,0:T(8,128)(2,1)S(1)}, u32[]{:S(2)}, u32[]{:S(2)}) %collective-permute-start.3) | collective-permute-done | bytes 262176 | tf_op jit(solution)/shard_map/ppermute | solution.py:521
  76.8 0.1 collective-permute-start.4
  76.9 1.9 %collective-permute-done.4.got_ref = bf16[16,128,128]{2,1,0:T(8,128)(2,1)S(1)} collective-permute-done((bf16[16,128,128]{2,1,0:T(8,128)(2,1)S(1)}, bf16[16,128,128]{2,1,0:T(8,128)(2,1)S(1)}, u32[]{:S(2)}, u32[]{:S(2)}) %collective-permute-start.4) | collective-permute-done | bytes 524320 | tf_op jit(solution)/shard_map/ppermute | solution.py:545
  78.8 0.2 merge.1
  79.0 24.7 %all_to_all.11.t_ref = bf16[16,384,128]{2,1,0:T(8,128)(2,1)S(1)} all-to-all(bf16[16,384,128]{2,1,0:T(8,128)(2,1)S(1)} %merge.1), channel_id=1, replica_groups=mesh['dp'=16,'ctx'=16] {'ctx'}, dimensions={0} | all-to-all | bytes 3145728 | tf_op jit(solution)/shard_map/all_to_all | solution.py:556
  103.8 1.9 %unpack.1 = (bf16[128,2048]{1,0:T(8,128)(2,1)}, bf16[128,2048]{1,0:T(8,128)(2,1)}, bf16[128,512]{1,0:T(8,128)(2,1)}, bf16[128,512]{1,0:T(8,128)(2,1)}) custom-call(bf16[16,384,128]{2,1,0:T(8,128)(2,1)S(1)} %all_to_all.11.t_ref), custom_call_target="tpu_custom_call" | custom-call | flops 800000000 | bytes 1048576 | tf_op jit(solution)/shard_map/unpack/pallas_call | solution.py:557
  (6 shorter events, 0.1 us)
Async XLA Ops:
  1.5 7.9 %collective-permute-start = (bf16[128,512]{1,0:T(8,128)(2,1)S(1)}, bf16[128,512]{1,0:T(8,128)(2,1)S(1)}, u32[]{:S(2)}, u32[]{:S(2)}) collective-permute-start(bf16[128,512]{1,0:T(8,128)(2,1)S(1)} %pad_maximum_fusion), channel_id=1, source_target_pairs={{0,16},{16,32},{32,48},{48,64},{64,80},{80,96},{96,112},{112,128},... | collective-permute-start | bytes 393224 | tf_op jit(solution)/shard_map/ppermute | solution.py:471
  43.3 2.4 %collective-permute-start.1 = (bf16[16,192,128]{2,1,0:T(8,128)(2,1)S(1)}, bf16[16,192,128]{2,1,0:T(8,128)(2,1)S(1)}, u32[]{:S(2)}, u32[]{:S(2)}) collective-permute-start(bf16[16,192,128]{2,1,0:T(8,128)(2,1)S(1)} %slice.20), channel_id=1, source_target_pairs={{0,1},{1,0},{2,3},{3,2},{4,5},{5,4},{6,7},{7,6},{8,9},{9,8},{10,11... | collective-permute-start | bytes 2359304 | tf_op jit(solution)/shard_map/ppermute | solution.py:497
  56.1 1.6 %collective-permute-start.2 = (bf16[16,64,128]{2,1,0:T(8,128)(2,1)S(1)}, bf16[16,64,128]{2,1,0:T(8,128)(2,1)S(1)}, u32[]{:S(2)}, u32[]{:S(2)}) collective-permute-start(bf16[16,64,128]{2,1,0:T(8,128)(2,1)S(1)} %get-tuple-element.28), channel_id=1, source_target_pairs={{0,1},{1,0},{2,3},{3,2},{4,5},{5,4},{6,7},{7,6},{8,9},{9,8},{10,11... | collective-permute-start | bytes 786440 | tf_op jit(solution)/shard_map/ppermute | solution.py:519
  57.8 19.0 %collective-permute-start.3 = (bf16[16,64,128]{2,1,0:T(8,128)(2,1)S(1)}, bf16[16,64,128]{2,1,0:T(8,128)(2,1)S(1)}, u32[]{:S(2)}, u32[]{:S(2)}) collective-permute-start(bf16[16,64,128]{2,1,0:T(8,128)(2,1)S(1)} %add_convert_fusion.after_ref), channel_id=1, source_target_pairs={{16,0},{32,16},{48,32},{64,48},{80,64},{96,80},{112,96},{128,112},... | collective-permute-start | bytes 786440 | tf_op jit(solution)/shard_map/ppermute | solution.py:521
  76.8 2.0 %collective-permute-start.4 = (bf16[16,128,128]{2,1,0:T(8,128)(2,1)S(1)}, bf16[16,128,128]{2,1,0:T(8,128)(2,1)S(1)}, u32[]{:S(2)}, u32[]{:S(2)}) collective-permute-start(bf16[16,128,128]{2,1,0:T(8,128)(2,1)S(1)} %tie.1), channel_id=1, source_target_pairs={{0,1},{1,0},{2,3},{3,2},{4,5},{5,4},{6,7},{7,6},{8,9},{9,8},{10,11... | collective-permute-start | bytes 1572872 | tf_op jit(solution)/shard_map/ppermute | solution.py:545
where the time goes:
time: 107 us; the launch traced here: 106 us
  blocking collectives  58.4 us (55%)
  Pallas kernels  25.9 us (24%)
  waiting for transfers between devices  11.2 us (10%)
  starting transfers between devices  7.42 us (7%)
    all_to_all x1, blocking collectives, on_device(): a = lax.all_to_all(a, 'ctx', 0, 0, tiled=True)  33.7 us
    all_to_all x1, blocking collectives, on_device(): out = lax.all_to_all(out, 'ctx', 0, 0, tiled=True)  24.7 us
    pallas_call x1, Pallas kernels, on_device(): call(own_kernel, 'own', 11, [SMEM, SMEM, VMEM, VMEM, VMEM, VMEM, VMEM, VM...  11.4 us
    pallas_call x1, Pallas kernels, on_device(): call(forward_kernel, 'forward', 16, [SMEM, VMEM, VMEM], [(VMEM, shape((QB...  10.5 us
    ppermute x1, waiting for transfers between devices, on_device(): sent_back = lax.ppermute(back, 'dp', [(i + 1, i) for i in range(15)])  5.59 us
    ppermute x1, starting transfers between devices, on_device(): tail = lax.ppermute(tail, 'dp', [(i, i + 1) for i in range(15)])  5.09 us
    ppermute x1, waiting for transfers between devices, on_device(): x = lax.ppermute(a[:, IN_X:IN_X + 192], 'ctx', swap)  2.18 us
  transfers between devices with their start and end apart: 5, of which 5 were waited for; matrix products, arithmetic and copies ran while one was open for 1% of the time, Pallas kernels for 13%

commit v1 on v0

--- a/solution.py
+++ b/solution.py
@@ -24,6 +24,7 @@
 SCALE = HEAD**-0.5
 FOLD = SCALE * 1.4426950408889634
 NEG = -1e30
+PIECES = 4
 BF = jnp.bfloat16
 F32 = jnp.float32
 
@@ -285,10 +286,11 @@
 
 def own_kernel(
     core_ref, plan_ref, a_ref, kv_ref, st_ref, lse_ref, delta_ref, dq_ref, old_ref, after_ref,
-    out_ref, keep_ref, give_ref,
-    vt_s, kt_s, acc_s, p_s, m_s, dq_s, o_s, dk_s, dv_s, sems,
+    out_ref, keep_ref, *rest,
 ):
     del old_ref, after_ref
+    give_refs, rest = rest[:PIECES], rest[PIECES:]
+    vt_s, kt_s, acc_s, p_s, m_s, dq_s, o_s, dk_s, dv_s, sems = rest
     core = core_ref[0]
     dk_s[...] = jnp.zeros_like(dk_s)
     dv_s[...] = jnp.zeros_like(dv_s)
@@ -367,18 +369,27 @@
         half, s0 = t // (OWN_TILES // 2), (t % (OWN_TILES // 2)) * KS
         at = (slice(s0, s0 + KS), slice(half * HALF, half * HALF + HALF))
         keep_ref[at] = jnp.where(even, dk, dv).astype(BF).reshape(KS, HALF, HEAD)
-        give_ref[at] = jnp.where(even, dv, dk).astype(BF).reshape(KS, HALF, HEAD)
+        given = jnp.where(even, dv, dk).astype(BF).reshape(KS, HALF, HEAD)
+        for b in range(KS):
+            piece, row = divmod(t * KS + b, 2 * MEMBERS // PIECES)
+            give_refs[piece][row] = given[b]
 
 
 def tie_kernel(x_ref, after_ref, o_ref, sems):
     del x_ref, after_ref, o_ref, sems
 
 
-def merge_kernel(keep_ref, got_ref, back_ref, old_ref, out_ref, x_s, sems):
-    lower, upper = slice(0, HALF), slice(HALF, 2 * HALF)
-    x_s[:, lower] = (keep_ref[:, lower].astype(F32) + got_ref[:, lower].astype(F32)).astype(BF)
-    total = keep_ref[:, upper].astype(F32) + got_ref[:, upper].astype(F32)
-    x_s[:, upper] = (total + back_ref[...].astype(F32)).astype(BF)
+def merge_kernel(keep_ref, back_ref, old_ref, *rest):
+    del old_ref
+    got_refs, (out_ref, x_s, sems) = rest[:PIECES], rest[PIECES:]
+    count = 2 * MEMBERS // PIECES
+    for piece, got_ref in enumerate(got_refs):
+        half, s0 = divmod(piece * count, MEMBERS)
+        at = (slice(s0, s0 + count), slice(half * HALF, half * HALF + HALF))
+        total = keep_ref[at].astype(F32) + got_ref[...].astype(F32)
+        if half == 1:
+            total = total + back_ref[s0 : s0 + count].astype(F32)
+        x_s[at] = total.astype(BF)
     finish(begin([(x_s, out_ref.at[:, pl.ds(OUT_X, 128)])], sems))
 
 
@@ -519,7 +530,7 @@
     got_back = lax.ppermute(give_back, "ctx", swap)
     back = (keep_back.astype(F32) + got_back.astype(F32)).astype(BF)
     sent_back = lax.ppermute(back, "dp", [(i + 1, i) for i in range(15)])
-    out, keep, give = call(
+    out, keep, *give = call(
         own_kernel,
         "own",
         11,
@@ -527,8 +538,8 @@
         [
             (HBM, shape((MEMBERS, OUT_ROWS, HEAD))),
             (VMEM, shape((MEMBERS, 128, HEAD))),
-            (VMEM, shape((MEMBERS, 128, HEAD))),
-        ],
+        ]
+        + [(VMEM, shape((2 * MEMBERS // PIECES, HALF, HEAD)))] * PIECES,
         [
             turned(BACK_TILES + OWN_TILES),
             turned(OWN_TILES),
@@ -542,17 +553,17 @@
         QB + 1,
         input_output_aliases={8: 0},
     )(which, plan, a, kv, st, lse, delta, dq, out, back)
-    got = lax.ppermute(tie(give, sent_back), "ctx", swap)
+    got = [lax.ppermute(each, "ctx", swap) for each in give]
     (out,) = call(
         merge_kernel,
         "merge",
         1,
-        [VMEM, VMEM, VMEM, HBM],
+        [VMEM, VMEM, HBM] + [VMEM] * PIECES,
         [(HBM, shape((MEMBERS, OUT_ROWS, HEAD)))],
         [pltpu.VMEM((MEMBERS, 128, HEAD), BF)],
         1,
-        input_output_aliases={3: 0},
-    )(keep, got, sent_back, out)
+        input_output_aliases={2: 0},
+    )(keep, sent_back, out, *got)
     out = lax.all_to_all(out, "ctx", 0, 0, tiled=True)
     attn, q_grad, k_grad, v_grad = call(
         unpack_kernel,

time: 107 us -> 105 us (0.981)
  the two profiles are of different devices: /device:TPU:6 before, /device:TPU:70 now
where the time goes in v1:
time: 105 us
  blocking collectives  54.7 us (52%)
  Pallas kernels  25.9 us (25%)
  waiting for transfers between devices  12 us (11%)
  starting transfers between devices  9.65 us (9%)
    all_to_all x1, blocking collectives, on_device(): a = lax.all_to_all(a, 'ctx', 0, 0, tiled=True)  30 us
    all_to_all x1, blocking collectives, on_device(): out = lax.all_to_all(out, 'ctx', 0, 0, tiled=True)  24.7 us
    pallas_call x1, Pallas kernels, on_device(): call(own_kernel, 'own', 11, [SMEM, SMEM, VMEM, VMEM, VMEM, VMEM, VMEM, VM...  11.4 us
    pallas_call x1, Pallas kernels, on_device(): call(forward_kernel, 'forward', 16, [SMEM, VMEM, VMEM], [(VMEM, shape((QB...  10.5 us
    ppermute x1, starting transfers between devices, on_device(): tail = lax.ppermute(tail, 'dp', [(i, i + 1) for i in range(15)])  6.3 us
    ppermute x1, waiting for transfers between devices, on_device(): sent_back = lax.ppermute(back, 'dp', [(i + 1, i) for i in range(15)])  4.6 us
    ppermute x1, waiting for transfers between devices, on_device(): tail = lax.ppermute(tail, 'dp', [(i, i + 1) for i in range(15)])  2.82 us
    ppermute x1, waiting for transfers between devices, on_device(): x = lax.ppermute(a[:, IN_X:IN_X + 192], 'ctx', swap)  2.18 us
  transfers between devices with their start and end apart: 8, of which 8 were waited for; matrix products, arithmetic and copies ran while one was open for 1% of the time, Pallas kernels for 13%

profile of v1, /device:TPU:70, one launch (start us, length us, event | category | flops | bytes accessed | tf_op | source)
XLA Modules:
  0.0 105.0 jit_solution(3642376136100380042)
XLA Ops:
  0.6 0.9 slice_bitcast_fusion
  1.5 6.3 %collective-permute-start = (bf16[128,512]{1,0:T(8,128)(2,1)S(1)}, bf16[128,512]{1,0:T(8,128)(2,1)S(1)}, u32[]{:S(2)}, u32[]{:S(2)}) collective-permute-start(bf16[128,512]{1,0:T(8,128)(2,1)S(1)} %pad_maximum_fusion), channel_id=1, source_target_pairs={{0,16},{16,32},{32,48},{48,64},{64,80},{80,96},{96,112},{112,128},... | collective-permute-start | bytes 393224 | tf_op jit(solution)/shard_map/ppermute | solution.py:482
  7.9 0.7 broadcast_subtract_fusion
  8.6 0.1 pad_select_fusion
  8.7 1.8 %pack.1.old_ref = bf16[16,464,128]{2,1,0:T(8,128)(2,1)S(1)} custom-call(bf16[128,2048]{1,0:T(8,128)(2,1)} %bitcast.24, bf16[128,2048]{1,0:T(8,128)(2,1)} %bitcast.25, bf16[128,512]{1,0:T(8,128)(2,1)} %bitcast.27, bf16[128,512]{1,0:T(8,128)(2,1)} %bitcast.26), custom_call_target="tpu_custom_call" | custom-call | flops 400000000 | bytes 1048576 | tf_op jit(solution)/shard_map/pack/pallas_call | solution.py:488
  10.5 2.8 %collective-permute-done.tail_ref = bf16[128,512]{1,0:T(8,128)(2,1)S(1)} collective-permute-done((bf16[128,512]{1,0:T(8,128)(2,1)S(1)}, bf16[128,512]{1,0:T(8,128)(2,1)S(1)}, u32[]{:S(2)}, u32[]{:S(2)}) %collective-permute-start) | collective-permute-done | bytes 131104 | tf_op jit(solution)/shard_map/ppermute | solution.py:482
  13.3 0.1 pack_tail.1
  13.4 30.0 %all_to_all.10.a_ref = bf16[16,464,128]{2,1,0:T(8,128)(2,1)S(1)} all-to-all(bf16[16,464,128]{2,1,0:T(8,128)(2,1)S(1)} %pack_tail.1), channel_id=1, replica_groups=mesh['dp'=16,'ctx'=16] {'ctx'}, dimensions={0} | all-to-all | bytes 3801088 | tf_op jit(solution)/shard_map/all_to_all | solution.py:507
  43.4 0.1 slice.20
  43.4 0.1 collective-permute-start.1
  43.6 0.1 pad_add_fusion.core_ref
  43.6 2.2 %collective-permute-done.1.x_ref = bf16[16,192,128]{2,1,0:T(8,128)(2,1)S(1)} collective-permute-done((bf16[16,192,128]{2,1,0:T(8,128)(2,1)S(1)}, bf16[16,192,128]{2,1,0:T(8,128)(2,1)S(1)}, u32[]{:S(2)}, u32[]{:S(2)}) %collective-permute-start.1) | collective-permute-done | bytes 786464 | tf_op jit(solution)/shard_map/ppermute | solution.py:508
  45.8 10.5 %forward.1 = (s32[4,1,512]{2,1,0:T(1,128)S(1)}, bf16[2,48,64,128]{3,2,1,0:T(8,128)(2,1)S(1)}, f32[4,1,512]{2,1,0:T(1,128)S(1)}, f32[4,1,512]{2,1,0:T(1,128)S(1)}...) custom-call(s32[2]{0:T(128)S(1)} %pad_add_fusion.core_ref, ...), custom_call_target="tpu_custom_call" | custom-call | flops 6400000000 | bytes 1048576 | tf_op jit(solution)/shard_map/forward/pallas_call | solution.py:509
  56.3 0.2 collective-permute-start.2
  56.5 1.4 %collective-permute-done.2 = bf16[16,64,128]{2,1,0:T(8,128)(2,1)S(1)} collective-permute-done((bf16[16,64,128]{2,1,0:T(8,128)(2,1)S(1)}, bf16[16,64,128]{2,1,0:T(8,128)(2,1)S(1)}, u32[]{:S(2)}, u32[]{:S(2)}) %collective-permute-start.2) | collective-permute-done | bytes 262176 | tf_op jit(solution)/shard_map/ppermute | solution.py:530
  57.9 0.1 add_convert_fusion.after_ref
  58.0 1.9 %collective-permute-start.3 = (bf16[16,64,128]{2,1,0:T(8,128)(2,1)S(1)}, bf16[16,64,128]{2,1,0:T(8,128)(2,1)S(1)}, u32[]{:S(2)}, u32[]{:S(2)}) collective-permute-start(bf16[16,64,128]{2,1,0:T(8,128)(2,1)S(1)} %add_convert_fusion.after_ref), channel_id=1, source_target_pairs={{16,0},{32,16},{48,32},{64,48},{80,64},{96,80},{112,96},{128,112},... | collective-permute-start | bytes 786440 | tf_op jit(solution)/shard_map/ppermute | solution.py:532
  59.9 11.4 %own.1 = (bf16[16,384,128]{2,1,0:T(8,128)(2,1)S(1)}, bf16[16,128,128]{2,1,0:T(8,128)(2,1)S(1)}, bf16[8,64,128]{2,1,0:T(8,128)(2,1)S(1)}, bf16[8,64,128]{2,1,0:T(...) custom-call(s32[2]{0:T(128)S(1)} %pad_add_fusion.core_ref, ...), custom_call_target="tpu_custom_call", output_to_operand_aliasing={{0}: (8, {})} | custom-call | flops 4400000000 | bytes 1048576 | tf_op jit(solution)/shard_map/own/pallas_call | solution.py:533
  71.4 0.2 collective-permute-start.4
  71.6 0.4 collective-permute-start.5
  72.0 0.1 collective-permute-start.6
  72.1 0.4 collective-permute-start.7
  72.5 0.3 collective-permute-done.4.rest_0_
  72.8 0.2 collective-permute-done.5.rest_1_
  73.0 0.3 collective-permute-done.6.rest_2_
  73.3 0.2 collective-permute-done.7.rest_3_
  73.5 4.6 %collective-permute-done.3.back_ref = bf16[16,64,128]{2,1,0:T(8,128)(2,1)S(1)} collective-permute-done((bf16[16,64,128]{2,1,0:T(8,128)(2,1)S(1)}, bf16[16,64,128]{2,1,0:T(8,128)(2,1)S(1)}, u32[]{:S(2)}, u32[]{:S(2)}) %collective-permute-start.3) | collective-permute-done | bytes 262176 | tf_op jit(solution)/shard_map/ppermute | solution.py:532
  78.1 0.2 merge.1
  78.3 24.7 %all_to_all.11.t_ref = bf16[16,384,128]{2,1,0:T(8,128)(2,1)S(1)} all-to-all(bf16[16,384,128]{2,1,0:T(8,128)(2,1)S(1)} %merge.1), channel_id=1, replica_groups=mesh['dp'=16,'ctx'=16] {'ctx'}, dimensions={0} | all-to-all | bytes 3145728 | tf_op jit(solution)/shard_map/all_to_all | solution.py:567
  103.1 1.9 %unpack.1 = (bf16[128,2048]{1,0:T(8,128)(2,1)}, bf16[128,2048]{1,0:T(8,128)(2,1)}, bf16[128,512]{1,0:T(8,128)(2,1)}, bf16[128,512]{1,0:T(8,128)(2,1)}) custom-call(bf16[16,384,128]{2,1,0:T(8,128)(2,1)S(1)} %all_to_all.11.t_ref), custom_call_target="tpu_custom_call" | custom-call | flops 800000000 | bytes 1048576 | tf_op jit(solution)/shard_map/unpack/pallas_call | solution.py:568
  (5 shorter events, 0.1 us)
Async XLA Ops:
  1.5 11.8 %collective-permute-start = (bf16[128,512]{1,0:T(8,128)(2,1)S(1)}, bf16[128,512]{1,0:T(8,128)(2,1)S(1)}, u32[]{:S(2)}, u32[]{:S(2)}) collective-permute-start(bf16[128,512]{1,0:T(8,128)(2,1)S(1)} %pad_maximum_fusion), channel_id=1, source_target_pairs={{0,16},{16,32},{32,48},{48,64},{64,80},{80,96},{96,112},{112,128},... | collective-permute-start | bytes 393224 | tf_op jit(solution)/shard_map/ppermute | solution.py:482
  43.4 2.4 %collective-permute-start.1 = (bf16[16,192,128]{2,1,0:T(8,128)(2,1)S(1)}, bf16[16,192,128]{2,1,0:T(8,128)(2,1)S(1)}, u32[]{:S(2)}, u32[]{:S(2)}) collective-permute-start(bf16[16,192,128]{2,1,0:T(8,128)(2,1)S(1)} %slice.20), channel_id=1, source_target_pairs={{0,1},{1,0},{2,3},{3,2},{4,5},{5,4},{6,7},{7,6},{8,9},{9,8},{10,11... | collective-permute-start | bytes 2359304 | tf_op jit(solution)/shard_map/ppermute | solution.py:508
  56.3 1.6 %collective-permute-start.2 = (bf16[16,64,128]{2,1,0:T(8,128)(2,1)S(1)}, bf16[16,64,128]{2,1,0:T(8,128)(2,1)S(1)}, u32[]{:S(2)}, u32[]{:S(2)}) collective-permute-start(bf16[16,64,128]{2,1,0:T(8,128)(2,1)S(1)} %get-tuple-element.31), channel_id=1, source_target_pairs={{0,1},{1,0},{2,3},{3,2},{4,5},{5,4},{6,7},{7,6},{8,9},{9,8},{10,11... | collective-permute-start | bytes 786440 | tf_op jit(solution)/shard_map/ppermute | solution.py:530
  58.0 20.1 %collective-permute-start.3 = (bf16[16,64,128]{2,1,0:T(8,128)(2,1)S(1)}, bf16[16,64,128]{2,1,0:T(8,128)(2,1)S(1)}, u32[]{:S(2)}, u32[]{:S(2)}) collective-permute-start(bf16[16,64,128]{2,1,0:T(8,128)(2,1)S(1)} %add_convert_fusion.after_ref), channel_id=1, source_target_pairs={{16,0},{32,16},{48,32},{64,48},{80,64},{96,80},{112,96},{128,112},... | collective-permute-start | bytes 786440 | tf_op jit(solution)/shard_map/ppermute | solution.py:532
  71.4 1.4 %collective-permute-start.4 = (bf16[8,64,128]{2,1,0:T(8,128)(2,1)S(1)}, bf16[8,64,128]{2,1,0:T(8,128)(2,1)S(1)}, u32[]{:S(2)}, u32[]{:S(2)}) collective-permute-start(bf16[8,64,128]{2,1,0:T(8,128)(2,1)S(1)} %get-tuple-element.34), channel_id=1, source_target_pairs={{0,1},{1,0},{2,3},{3,2},{4,5},{5,4},{6,7},{7,6},{8,9},{9,8},{10,11... | collective-permute-start | bytes 393224 | tf_op jit(solution)/shard_map/ppermute | solution.py:556
  71.6 1.4 %collective-permute-start.5 = (bf16[8,64,128]{2,1,0:T(8,128)(2,1)S(1)}, bf16[8,64,128]{2,1,0:T(8,128)(2,1)S(1)}, u32[]{:S(2)}, u32[]{:S(2)}) collective-permute-start(bf16[8,64,128]{2,1,0:T(8,128)(2,1)S(1)} %get-tuple-element.35), channel_id=1, source_target_pairs={{0,1},{1,0},{2,3},{3,2},{4,5},{5,4},{6,7},{7,6},{8,9},{9,8},{10,11... | collective-permute-start | bytes 393224 | tf_op jit(solution)/shard_map/ppermute | solution.py:556
  72.0 1.3 %collective-permute-start.6 = (bf16[8,64,128]{2,1,0:T(8,128)(2,1)S(1)}, bf16[8,64,128]{2,1,0:T(8,128)(2,1)S(1)}, u32[]{:S(2)}, u32[]{:S(2)}) collective-permute-start(bf16[8,64,128]{2,1,0:T(8,128)(2,1)S(1)} %get-tuple-element.36), channel_id=1, source_target_pairs={{0,1},{1,0},{2,3},{3,2},{4,5},{5,4},{6,7},{7,6},{8,9},{9,8},{10,11... | collective-permute-start | bytes 393224 | tf_op jit(solution)/shard_map/ppermute | solution.py:556
  72.1 1.4 %collective-permute-start.7 = (bf16[8,64,128]{2,1,0:T(8,128)(2,1)S(1)}, bf16[8,64,128]{2,1,0:T(8,128)(2,1)S(1)}, u32[]{:S(2)}, u32[]{:S(2)}) collective-permute-start(bf16[8,64,128]{2,1,0:T(8,128)(2,1)S(1)} %get-tuple-element.37), channel_id=1, source_target_pairs={{0,1},{1,0},{2,3},{3,2},{4,5},{5,4},{6,7},{7,6},{8,9},{9,8},{10,11... | collective-permute-start | bytes 393224 | tf_op jit(solution)/shard_map/ppermute | solution.py:556

commit v2 on v1

--- a/solution.py
+++ b/solution.py
@@ -55,23 +55,26 @@
     return pl.ds(n * HEAD, HEAD)
 
 
-def pack_kernel(q_ref, g_ref, k_ref, v_ref, o_ref, sems):
+def pack_kernel(q_ref, g_ref, k_ref, v_ref, s_ref, o_ref, sems):
     pairs = []
     for n in range(HEADS):
         x_ref = k_ref if n % 2 == 0 else v_ref
         pairs.append((q_ref.at[:, columns(n)], o_ref.at[n, pl.ds(IN_Q, 128)]))
         pairs.append((g_ref.at[:, columns(n)], o_ref.at[n, pl.ds(IN_G, 128)]))
         pairs.append((x_ref.at[:, columns(n // 4)], o_ref.at[n, pl.ds(IN_X, 128)]))
+    copies = begin(pairs, sems)
+    for n in range(HEADS):
+        o_ref[n, IN_S : IN_S + 16] = s_ref[...]
+    finish(copies)
+
+
+def pack_tail_kernel(tail_ref, old_ref, o_ref, sems):
+    del old_ref
+    pairs = []
+    for n in range(HEADS):
+        rows = pl.ds((n % 2) * HALF, HALF)
+        pairs.append((tail_ref.at[rows, columns(n // 4)], o_ref.at[n, pl.ds(IN_X + 128, HALF)]))
     finish(begin(pairs, sems))
-
-
-def pack_tail_kernel(tail_ref, s_ref, old_ref, o_ref, x_s, sems):
-    del old_ref
-    for n in range(HEADS):
-        row = (n % 2) * HALF
-        x_s[n, 0:HALF] = tail_ref[row : row + HALF, n // 4 * HEAD : (n // 4 + 1) * HEAD]
-        x_s[n, HALF : HALF + 16] = s_ref[...]
-    finish(begin([(x_s, o_ref.at[:, pl.ds(IN_X + 128, HALF + 16)])], sems))
 
 
 def low_position(i):
@@ -379,33 +382,42 @@
     del x_ref, after_ref, o_ref, sems
 
 
-def merge_kernel(keep_ref, back_ref, old_ref, *rest):
+def merge_kernel(keep_ref, old_ref, *rest):
     del old_ref
-    got_refs, (out_ref, x_s, sems) = rest[:PIECES], rest[PIECES:]
+    got_refs, (out_ref, upper_ref, x_s, sems) = rest[:PIECES], rest[PIECES:]
     count = 2 * MEMBERS // PIECES
     for piece, got_ref in enumerate(got_refs):
         half, s0 = divmod(piece * count, MEMBERS)
         at = (slice(s0, s0 + count), slice(half * HALF, half * HALF + HALF))
         total = keep_ref[at].astype(F32) + got_ref[...].astype(F32)
-        if half == 1:
-            total = total + back_ref[s0 : s0 + count].astype(F32)
-        x_s[at] = total.astype(BF)
-    finish(begin([(x_s, out_ref.at[:, pl.ds(OUT_X, 128)])], sems))
-
-
-def unpack_kernel(t_ref, a_ref, q_ref, k_ref, v_ref, sems):
+        if half == 0:
+            x_s[s0 : s0 + count] = total.astype(BF)
+        else:
+            upper_ref[s0 : s0 + count] = total
+    finish(begin([(x_s, out_ref.at[:, pl.ds(OUT_X, HALF)])], sems))
+
+
+def merge_back_kernel(upper_ref, back_ref, old_ref, out_ref, x_s, sems):
+    del old_ref
+    x_s[...] = (upper_ref[...] + back_ref[...].astype(F32)).astype(BF)
+    finish(begin([(x_s, out_ref.at[:, pl.ds(OUT_X + HALF, HALF)])], sems))
+
+
+def unpack_kernel(t_ref, a_ref, q_ref, k_ref, v_ref, k_s, v_s, sems):
     pairs = []
     for n in range(HEADS):
         pairs.append((t_ref.at[n, pl.ds(OUT_A, 128)], a_ref.at[:, columns(n)]))
         pairs.append((t_ref.at[n, pl.ds(OUT_Q, 128)], q_ref.at[:, columns(n)]))
     copies = begin(pairs, sems)
-    for g in range(GROUPS):
-        at = slice(g * HEAD, (g + 1) * HEAD)
-        for n, o_ref in ((4 * g, k_ref), (4 * g + 1, v_ref)):
+    for index, (n0, o_s, o_ref) in enumerate(((0, k_s, k_ref), (1, v_s, v_ref))):
+        for g in range(GROUPS):
+            n = 4 * g + n0
             total = t_ref[n, OUT_X : OUT_X + 128].astype(F32) + t_ref[
                 n + 2, OUT_X : OUT_X + 128
             ].astype(F32)
-            o_ref[:, at] = total.astype(BF)
+            o_s[:, g * HEAD : (g + 1) * HEAD] = total.astype(BF)
+        copies.append(pltpu.make_async_copy(o_s, o_ref, sems.at[2 * HEADS + index]))
+        copies[-1].start()
     finish(copies)
 
 
@@ -489,21 +501,21 @@
         pack_kernel,
         "pack",
         1,
-        [HBM, HBM, HBM, HBM],
+        [HBM, HBM, HBM, HBM, VMEM],
         [(VMEM, packets)],
         [],
         3 * HEADS,
-    )(*(pltpu.with_memory_space_constraint(each, pltpu.HBM) for each in (q, g, k, v)))
+    )(*(pltpu.with_memory_space_constraint(each, pltpu.HBM) for each in (q, g, k, v)), starts)
     (a,) = call(
         pack_tail_kernel,
         "pack_tail",
         1,
-        [VMEM, VMEM, pl.BlockSpec(memory_space=pl.ANY)],
+        [VMEM, pl.BlockSpec(memory_space=pl.ANY)],
         [(pl.BlockSpec(memory_space=pl.ANY), packets)],
-        [pltpu.VMEM((HEADS, HALF + 16, HEAD), BF)],
-        1,
-        input_output_aliases={2: 0},
-    )(tail, starts, a)
+        [],
+        HEADS,
+        input_output_aliases={1: 0},
+    )(tail, a)
     a = lax.all_to_all(a, "ctx", 0, 0, tiled=True)
     x = lax.ppermute(a[:, IN_X : IN_X + 192], "ctx", swap)
     st, kv, lse, delta, out, dq, keep_back, give_back, plan = call(
@@ -554,25 +566,35 @@
         input_output_aliases={8: 0},
     )(which, plan, a, kv, st, lse, delta, dq, out, back)
     got = [lax.ppermute(each, "ctx", swap) for each in give]
-    (out,) = call(
+    out, upper = call(
         merge_kernel,
         "merge",
         1,
-        [VMEM, VMEM, HBM] + [VMEM] * PIECES,
+        [VMEM, HBM] + [VMEM] * PIECES,
+        [(HBM, shape((MEMBERS, OUT_ROWS, HEAD))), (VMEM, shape((MEMBERS, HALF, HEAD), F32))],
+        [pltpu.VMEM((MEMBERS, HALF, HEAD), BF)],
+        1,
+        input_output_aliases={1: 0},
+    )(keep, out, *got)
+    (out,) = call(
+        merge_back_kernel,
+        "merge_back",
+        1,
+        [VMEM, VMEM, HBM],
         [(HBM, shape((MEMBERS, OUT_ROWS, HEAD)))],
-        [pltpu.VMEM((MEMBERS, 128, HEAD), BF)],
+        [pltpu.VMEM((MEMBERS, HALF, HEAD), BF)],
         1,
         input_output_aliases={2: 0},
-    )(keep, sent_back, out, *got)
+    )(upper, sent_back, out)
     out = lax.all_to_all(out, "ctx", 0, 0, tiled=True)
     attn, q_grad, k_grad, v_grad = call(
         unpack_kernel,
         "unpack",
         2,
         [VMEM],
-        [(HBM, shape(q.shape)), (HBM, shape(q.shape)), (VMEM, shape(k.shape)), (VMEM, shape(k.shape))],
-        [],
-        2 * HEADS,
+        [(HBM, shape(q.shape)), (HBM, shape(q.shape)), (HBM, shape(k.shape)), (HBM, shape(k.shape))],
+        [pltpu.VMEM(k.shape, BF), pltpu.VMEM(k.shape, BF)],
+        2 * HEADS + 2,
     )(out)
     return (
         attn.reshape(queries.shape),

time: 105 us -> 105 us (level)
    pallas_call x3 -> x4, Pallas kernels: 2.06 us -> 2.22 us  [the longest x1 1.79 us: on_device(): call(pack_kernel, 'pack', 1, [HBM, HBM, HBM, HBM, VMEM], [(VMEM, packets)...]
where the time goes in v2:
time: 105 us; the launch traced here: 104 us
  blocking collectives  54.7 us (52%)
  Pallas kernels  25.5 us (24%)
  waiting for transfers between devices  11.8 us (11%)
  starting transfers between devices  9.65 us (9%)
    all_to_all x1, blocking collectives, on_device(): a = lax.all_to_all(a, 'ctx', 0, 0, tiled=True)  30 us
    all_to_all x1, blocking collectives, on_device(): out = lax.all_to_all(out, 'ctx', 0, 0, tiled=True)  24.7 us
    pallas_call x1, Pallas kernels, on_device(): call(own_kernel, 'own', 11, [SMEM, SMEM, VMEM, VMEM, VMEM, VMEM, VMEM, VM...  11.4 us
    pallas_call x1, Pallas kernels, on_device(): call(forward_kernel, 'forward', 16, [SMEM, VMEM, VMEM], [(VMEM, shape((QB...  10.5 us
    ppermute x1, starting transfers between devices, on_device(): tail = lax.ppermute(tail, 'dp', [(i, i + 1) for i in range(15)])  6.3 us
    ppermute x1, waiting for transfers between devices, on_device(): sent_back = lax.ppermute(back, 'dp', [(i + 1, i) for i in range(15)])  4.41 us
    ppermute x1, waiting for transfers between devices, on_device(): tail = lax.ppermute(tail, 'dp', [(i, i + 1) for i in range(15)])  2.82 us
    ppermute x1, waiting for transfers between devices, on_device(): x = lax.ppermute(a[:, IN_X:IN_X + 192], 'ctx', swap)  2.18 us
  transfers between devices with their start and end apart: 8, of which 8 were waited for; matrix products, arithmetic and copies ran while one was open for 1% of the time, Pallas kernels for 13%

profile of v2, /device:TPU:70, one launch (start us, length us, event | category | flops | bytes accessed | tf_op | source)
XLA Modules:
  0.0 104.4 jit_solution(15712630796668048490)
XLA Ops:
  0.6 0.9 slice_bitcast_fusion
  1.5 6.3 %collective-permute-start = (bf16[128,512]{1,0:T(8,128)(2,1)S(1)}, bf16[128,512]{1,0:T(8,128)(2,1)S(1)}, u32[]{:S(2)}, u32[]{:S(2)}) collective-permute-start(bf16[128,512]{1,0:T(8,128)(2,1)S(1)} %pad_maximum_fusion), channel_id=1, source_target_pairs={{0,16},{16,32},{32,48},{48,64},{64,80},{80,96},{96,112},{112,128},... | collective-permute-start | bytes 393224 | tf_op jit(solution)/shard_map/ppermute | solution.py:494
  7.9 0.7 broadcast_subtract_fusion
  8.6 0.1 pad_select_fusion
  8.7 1.8 %pack.1.old_ref = bf16[16,464,128]{2,1,0:T(8,128)(2,1)S(1)} custom-call(bf16[128,2048]{1,0:T(8,128)(2,1)} %bitcast.24, bf16[128,2048]{1,0:T(8,128)(2,1)} %bitcast.25, bf16[128,512]{1,0:T(8,128)(2,1)} %bitcast.27, bf16[128,512]{1,0:T(8,128)(2,1)} %bitcast.26, bf16[16,128]{1,0:T(8,128)(2,1)S(1)} %pad.6.s_ref), custom_call_target="tpu_custom_call" | custom-call | flops 400000000 | bytes 1048576 | tf_op jit(solution)/shard_map/pack/pallas_call | solution.py:500
  10.5 2.8 %collective-permute-done.tail_ref = bf16[128,512]{1,0:T(8,128)(2,1)S(1)} collective-permute-done((bf16[128,512]{1,0:T(8,128)(2,1)S(1)}, bf16[128,512]{1,0:T(8,128)(2,1)S(1)}, u32[]{:S(2)}, u32[]{:S(2)}) %collective-permute-start) | collective-permute-done | bytes 131104 | tf_op jit(solution)/shard_map/ppermute | solution.py:494
  13.3 0.2 pack_tail.1
  13.5 30.0 %all_to_all.10.a_ref = bf16[16,464,128]{2,1,0:T(8,128)(2,1)S(1)} all-to-all(bf16[16,464,128]{2,1,0:T(8,128)(2,1)S(1)} %pack_tail.1), channel_id=1, replica_groups=mesh['dp'=16,'ctx'=16] {'ctx'}, dimensions={0} | all-to-all | bytes 3801088 | tf_op jit(solution)/shard_map/all_to_all | solution.py:519
  43.5 0.1 slice.20
  43.6 0.1 collective-permute-start.1
  43.7 0.1 pad_add_fusion.core_ref
  43.8 2.2 %collective-permute-done.1.x_ref = bf16[16,192,128]{2,1,0:T(8,128)(2,1)S(1)} collective-permute-done((bf16[16,192,128]{2,1,0:T(8,128)(2,1)S(1)}, bf16[16,192,128]{2,1,0:T(8,128)(2,1)S(1)}, u32[]{:S(2)}, u32[]{:S(2)}) %collective-permute-start.1) | collective-permute-done | bytes 786464 | tf_op jit(solution)/shard_map/ppermute | solution.py:520
  46.0 10.5 %forward.1 = (s32[4,1,512]{2,1,0:T(1,128)S(1)}, bf16[2,48,64,128]{3,2,1,0:T(8,128)(2,1)S(1)}, f32[4,1,512]{2,1,0:T(1,128)S(1)}, f32[4,1,512]{2,1,0:T(1,128)S(1)}...) custom-call(s32[2]{0:T(128)S(1)} %pad_add_fusion.core_ref, ...), custom_call_target="tpu_custom_call" | custom-call | flops 6400000000 | bytes 1048576 | tf_op jit(solution)/shard_map/forward/pallas_call | solution.py:521
  56.4 0.2 collective-permute-start.2
  56.7 1.4 %collective-permute-done.2 = bf16[16,64,128]{2,1,0:T(8,128)(2,1)S(1)} collective-permute-done((bf16[16,64,128]{2,1,0:T(8,128)(2,1)S(1)}, bf16[16,64,128]{2,1,0:T(8,128)(2,1)S(1)}, u32[]{:S(2)}, u32[]{:S(2)}) %collective-permute-start.2) | collective-permute-done | bytes 262176 | tf_op jit(solution)/shard_map/ppermute | solution.py:542
  58.1 0.1 add_convert_fusion.after_ref
  58.1 1.9 %collective-permute-start.7 = (bf16[16,64,128]{2,1,0:T(8,128)(2,1)S(1)}, bf16[16,64,128]{2,1,0:T(8,128)(2,1)S(1)}, u32[]{:S(2)}, u32[]{:S(2)}) collective-permute-start(bf16[16,64,128]{2,1,0:T(8,128)(2,1)S(1)} %add_convert_fusion.after_ref), channel_id=1, source_target_pairs={{16,0},{32,16},{48,32},{64,48},{80,64},{96,80},{112,96},{128,112},... | collective-permute-start | bytes 786440 | tf_op jit(solution)/shard_map/ppermute | solution.py:544
  60.1 11.4 %own.1 = (bf16[16,384,128]{2,1,0:T(8,128)(2,1)S(1)}, bf16[16,128,128]{2,1,0:T(8,128)(2,1)S(1)}, bf16[8,64,128]{2,1,0:T(8,128)(2,1)S(1)}, bf16[8,64,128]{2,1,0:T(...) custom-call(s32[2]{0:T(128)S(1)} %pad_add_fusion.core_ref, ...), custom_call_target="tpu_custom_call", output_to_operand_aliasing={{0}: (8, {})} | custom-call | flops 4400000000 | bytes 1048576 | tf_op jit(solution)/shard_map/own/pallas_call | solution.py:545
  71.5 0.2 collective-permute-start.3
  71.7 0.4 collective-permute-start.4
  72.1 0.1 collective-permute-start.5
  72.3 0.4 collective-permute-start.6
  72.6 0.3 collective-permute-done.3.rest_0_
  73.0 0.2 collective-permute-done.4.rest_1_
  73.1 0.3 collective-permute-done.5.rest_2_
  73.5 0.2 collective-permute-done.6.rest_3_
  73.7 0.1 merge.1
  73.8 4.4 %collective-permute-done.7.back_ref = bf16[16,64,128]{2,1,0:T(8,128)(2,1)S(1)} collective-permute-done((bf16[16,64,128]{2,1,0:T(8,128)(2,1)S(1)}, bf16[16,64,128]{2,1,0:T(8,128)(2,1)S(1)}, u32[]{:S(2)}, u32[]{:S(2)}) %collective-permute-start.7) | collective-permute-done | bytes 262176 | tf_op jit(solution)/shard_map/ppermute | solution.py:544
  78.2 0.1 merge_back.1
  78.3 24.7 %all_to_all.11.t_ref = bf16[16,384,128]{2,1,0:T(8,128)(2,1)S(1)} all-to-all(bf16[16,384,128]{2,1,0:T(8,128)(2,1)S(1)} %merge_back.1), channel_id=1, replica_groups=mesh['dp'=16,'ctx'=16] {'ctx'}, dimensions={0} | all-to-all | bytes 3145728 | tf_op jit(solution)/shard_map/all_to_all | solution.py:589
  103.0 1.3 %unpack.1 = (bf16[128,2048]{1,0:T(8,128)(2,1)}, bf16[128,2048]{1,0:T(8,128)(2,1)}, bf16[128,512]{1,0:T(8,128)(2,1)}, bf16[128,512]{1,0:T(8,128)(2,1)}) custom-call(bf16[16,384,128]{2,1,0:T(8,128)(2,1)S(1)} %all_to_all.11.t_ref), custom_call_target="tpu_custom_call" | custom-call | flops 800000000 | bytes 1048576 | tf_op jit(solution)/shard_map/unpack/pallas_call | solution.py:590
  (5 shorter events, 0.1 us)
Async XLA Ops:
  1.5 11.8 %collective-permute-start = (bf16[128,512]{1,0:T(8,128)(2,1)S(1)}, bf16[128,512]{1,0:T(8,128)(2,1)S(1)}, u32[]{:S(2)}, u32[]{:S(2)}) collective-permute-start(bf16[128,512]{1,0:T(8,128)(2,1)S(1)} %pad_maximum_fusion), channel_id=1, source_target_pairs={{0,16},{16,32},{32,48},{48,64},{64,80},{80,96},{96,112},{112,128},... | collective-permute-start | bytes 393224 | tf_op jit(solution)/shard_map/ppermute | solution.py:494
  43.6 2.4 %collective-permute-start.1 = (bf16[16,192,128]{2,1,0:T(8,128)(2,1)S(1)}, bf16[16,192,128]{2,1,0:T(8,128)(2,1)S(1)}, u32[]{:S(2)}, u32[]{:S(2)}) collective-permute-start(bf16[16,192,128]{2,1,0:T(8,128)(2,1)S(1)} %slice.20), channel_id=1, source_target_pairs={{0,1},{1,0},{2,3},{3,2},{4,5},{5,4},{6,7},{7,6},{8,9},{9,8},{10,11... | collective-permute-start | bytes 2359304 | tf_op jit(solution)/shard_map/ppermute | solution.py:520
  56.4 1.6 %collective-permute-start.2 = (bf16[16,64,128]{2,1,0:T(8,128)(2,1)S(1)}, bf16[16,64,128]{2,1,0:T(8,128)(2,1)S(1)}, u32[]{:S(2)}, u32[]{:S(2)}) collective-permute-start(bf16[16,64,128]{2,1,0:T(8,128)(2,1)S(1)} %get-tuple-element.33), channel_id=1, source_target_pairs={{0,1},{1,0},{2,3},{3,2},{4,5},{5,4},{6,7},{7,6},{8,9},{9,8},{10,11... | collective-permute-start | bytes 786440 | tf_op jit(solution)/shard_map/ppermute | solution.py:542
  58.1 20.1 %collective-permute-start.7 = (bf16[16,64,128]{2,1,0:T(8,128)(2,1)S(1)}, bf16[16,64,128]{2,1,0:T(8,128)(2,1)S(1)}, u32[]{:S(2)}, u32[]{:S(2)}) collective-permute-start(bf16[16,64,128]{2,1,0:T(8,128)(2,1)S(1)} %add_convert_fusion.after_ref), channel_id=1, source_target_pairs={{16,0},{32,16},{48,32},{64,48},{80,64},{96,80},{112,96},{128,112},... | collective-permute-start | bytes 786440 | tf_op jit(solution)/shard_map/ppermute | solution.py:544
  71.5 1.4 %collective-permute-start.3 = (bf16[8,64,128]{2,1,0:T(8,128)(2,1)S(1)}, bf16[8,64,128]{2,1,0:T(8,128)(2,1)S(1)}, u32[]{:S(2)}, u32[]{:S(2)}) collective-permute-start(bf16[8,64,128]{2,1,0:T(8,128)(2,1)S(1)} %get-tuple-element.36), channel_id=1, source_target_pairs={{0,1},{1,0},{2,3},{3,2},{4,5},{5,4},{6,7},{7,6},{8,9},{9,8},{10,11... | collective-permute-start | bytes 393224 | tf_op jit(solution)/shard_map/ppermute | solution.py:568
  71.7 1.4 %collective-permute-start.4 = (bf16[8,64,128]{2,1,0:T(8,128)(2,1)S(1)}, bf16[8,64,128]{2,1,0:T(8,128)(2,1)S(1)}, u32[]{:S(2)}, u32[]{:S(2)}) collective-permute-start(bf16[8,64,128]{2,1,0:T(8,128)(2,1)S(1)} %get-tuple-element.37), channel_id=1, source_target_pairs={{0,1},{1,0},{2,3},{3,2},{4,5},{5,4},{6,7},{7,6},{8,9},{9,8},{10,11... | collective-permute-start | bytes 393224 | tf_op jit(solution)/shard_map/ppermute | solution.py:568
  72.1 1.3 %collective-permute-start.5 = (bf16[8,64,128]{2,1,0:T(8,128)(2,1)S(1)}, bf16[8,64,128]{2,1,0:T(8,128)(2,1)S(1)}, u32[]{:S(2)}, u32[]{:S(2)}) collective-permute-start(bf16[8,64,128]{2,1,0:T(8,128)(2,1)S(1)} %get-tuple-element.38), channel_id=1, source_target_pairs={{0,1},{1,0},{2,3},{3,2},{4,5},{5,4},{6,7},{7,6},{8,9},{9,8},{10,11... | collective-permute-start | bytes 393224 | tf_op jit(solution)/shard_map/ppermute | solution.py:568
  72.3 1.4 %collective-permute-start.6 = (bf16[8,64,128]{2,1,0:T(8,128)(2,1)S(1)}, bf16[8,64,128]{2,1,0:T(8,128)(2,1)S(1)}, u32[]{:S(2)}, u32[]{:S(2)}) collective-permute-start(bf16[8,64,128]{2,1,0:T(8,128)(2,1)S(1)} %get-tuple-element.39), channel_id=1, source_target_pairs={{0,1},{1,0},{2,3},{3,2},{4,5},{5,4},{6,7},{7,6},{8,9},{9,8},{10,11... | collective-permute-start | bytes 393224 | tf_op jit(solution)/shard_map/ppermute | solution.py:568

commit v3 on v2

--- a/solution.py
+++ b/solution.py
@@ -224,7 +224,8 @@
         start = both[row : row + 1] * 64.0 + both[row + 1 : row + 2]
         c = (t % 4) * 128
         st_ref[t // 4, 0:1, c : c + 128] = start.astype(jnp.int32)
-    for t in range(BACK_TILES + OWN_TILES):
+    lower = BACK_TILES + OWN_TILES // 2
+    for t in range(lower):
         vt_s[t] = rows_of(kv_s.at[1], t, KS).T
     for t in range(BACK_TILES):
         kt_s[t] = rows_of(kv_s.at[0], t, KS).T
@@ -246,6 +247,11 @@
         extra = (first >= BACK_TILES) & (need <= budget)
         budget -= jnp.where(extra, need, 0)
         plan_ref[i] = ((first < BACK_TILES) | extra).astype(jnp.int32)
+
+    @pl.when(plan_ref[QB // 2] + plan_ref[QB // 2 + 1] > 0)
+    def _():
+        for t in range(lower, BACK_TILES + OWN_TILES):
+            vt_s[t] = rows_of(kv_s.at[1], t, KS).T
 
     def q_block(i, _):
         @pl.when(plan_ref[i] == 1)
@@ -468,7 +474,7 @@
     k = key_states.reshape(128, GROUPS * HEAD)
     v = value_vectors.reshape(128, GROUPS * HEAD)
     swap = [(i, i ^ 1) for i in range(MEMBERS)]
-    budget = jnp.where(cycle % 4 == 0, 0, jnp.where(cycle % 4 == 1, 64, 40))
+    budget = jnp.where(cycle % 4 == 0, 0, jnp.where(cycle % 4 == 3, 16, 56))
     which = jnp.stack([core, budget])
 
     rel = doc_start.reshape(2, HALF) - (cycle * SPAN - BACK)

time: 105 us -> 105 us (level)
  waiting for transfers between devices: 11.8 us -> 15.5 us
  Pallas kernels: 25.5 us -> 22.5 us
    ppermute x1, waiting for transfers between devices: 4.41 us -> 8.06 us  [on_device(): sent_back = lax.ppermute(back, 'dp', [(i + 1, i) for i in range(15)])]
    pallas_call x1, Pallas kernels: 10.5 us -> 7.48 us  [on_device(): call(forward_kernel, 'forward', 16, [SMEM, VMEM, VMEM], [(VMEM, shape((QB...]
where the time goes in v3:
time: 105 us
  blocking collectives  54.7 us (52%)
  Pallas kernels  22.5 us (21%)
  waiting for transfers between devices  15.5 us (15%)
  starting transfers between devices  9.74 us (9%)
    all_to_all x1, blocking collectives, on_device(): a = lax.all_to_all(a, 'ctx', 0, 0, tiled=True)  30 us
    all_to_all x1, blocking collectives, on_device(): out = lax.all_to_all(out, 'ctx', 0, 0, tiled=True)  24.7 us
    pallas_call x1, Pallas kernels, on_device(): call(own_kernel, 'own', 11, [SMEM, SMEM, VMEM, VMEM, VMEM, VMEM, VMEM, VM...  11.4 us
    ppermute x1, waiting for transfers between devices, on_device(): sent_back = lax.ppermute(back, 'dp', [(i + 1, i) for i in range(15)])  8.06 us
    pallas_call x1, Pallas kernels, on_device(): call(forward_kernel, 'forward', 16, [SMEM, VMEM, VMEM], [(VMEM, shape((QB...  7.48 us
    ppermute x1, starting transfers between devices, on_device(): tail = lax.ppermute(tail, 'dp', [(i, i + 1) for i in range(15)])  6.3 us
    ppermute x1, waiting for transfers between devices, on_device(): tail = lax.ppermute(tail, 'dp', [(i, i + 1) for i in range(15)])  2.82 us
    ppermute x1, waiting for transfers between devices, on_device(): x = lax.ppermute(a[:, IN_X:IN_X + 192], 'ctx', swap)  2.18 us
  transfers between devices with their start and end apart: 8, of which 8 were waited for; matrix products, arithmetic and copies ran while one was open for 1% of the time, Pallas kernels for 13%

profile of v3, /device:TPU:70, one launch (start us, length us, event | category | flops | bytes accessed | tf_op | source)
XLA Modules:
  0.0 105.1 jit_solution(1612615979892908510)
XLA Ops:
  0.6 0.9 slice_bitcast_fusion
  1.5 6.3 %collective-permute-start = (bf16[128,512]{1,0:T(8,128)(2,1)S(1)}, bf16[128,512]{1,0:T(8,128)(2,1)S(1)}, u32[]{:S(2)}, u32[]{:S(2)}) collective-permute-start(bf16[128,512]{1,0:T(8,128)(2,1)S(1)} %pad_maximum_fusion), channel_id=1, source_target_pairs={{0,16},{16,32},{32,48},{48,64},{64,80},{80,96},{96,112},{112,128},... | collective-permute-start | bytes 393224 | tf_op jit(solution)/shard_map/ppermute | solution.py:500
  7.9 0.7 broadcast_subtract_fusion
  8.6 0.1 pad_select_fusion
  8.7 1.8 %pack.1.old_ref = bf16[16,464,128]{2,1,0:T(8,128)(2,1)S(1)} custom-call(bf16[128,2048]{1,0:T(8,128)(2,1)} %bitcast.24, bf16[128,2048]{1,0:T(8,128)(2,1)} %bitcast.25, bf16[128,512]{1,0:T(8,128)(2,1)} %bitcast.27, bf16[128,512]{1,0:T(8,128)(2,1)} %bitcast.26, bf16[16,128]{1,0:T(8,128)(2,1)S(1)} %pad.6.s_ref), custom_call_target="tpu_custom_call" | custom-call | flops 400000000 | bytes 1048576 | tf_op jit(solution)/shard_map/pack/pallas_call | solution.py:506
  10.5 2.8 %collective-permute-done.tail_ref = bf16[128,512]{1,0:T(8,128)(2,1)S(1)} collective-permute-done((bf16[128,512]{1,0:T(8,128)(2,1)S(1)}, bf16[128,512]{1,0:T(8,128)(2,1)S(1)}, u32[]{:S(2)}, u32[]{:S(2)}) %collective-permute-start) | collective-permute-done | bytes 131104 | tf_op jit(solution)/shard_map/ppermute | solution.py:500
  13.3 0.2 pack_tail.1
  13.5 30.0 %all_to_all.10.a_ref = bf16[16,464,128]{2,1,0:T(8,128)(2,1)S(1)} all-to-all(bf16[16,464,128]{2,1,0:T(8,128)(2,1)S(1)} %pack_tail.1), channel_id=1, replica_groups=mesh['dp'=16,'ctx'=16] {'ctx'}, dimensions={0} | all-to-all | bytes 3801088 | tf_op jit(solution)/shard_map/all_to_all | solution.py:525
  43.5 0.1 slice.20
  43.6 0.1 collective-permute-start.1
  43.7 0.1 pad_add_fusion.core_ref
  43.8 2.2 %collective-permute-done.1.x_ref = bf16[16,192,128]{2,1,0:T(8,128)(2,1)S(1)} collective-permute-done((bf16[16,192,128]{2,1,0:T(8,128)(2,1)S(1)}, bf16[16,192,128]{2,1,0:T(8,128)(2,1)S(1)}, u32[]{:S(2)}, u32[]{:S(2)}) %collective-permute-start.1) | collective-permute-done | bytes 786464 | tf_op jit(solution)/shard_map/ppermute | solution.py:526
  46.0 7.5 %forward.1 = (s32[4,1,512]{2,1,0:T(1,128)S(1)}, bf16[2,48,64,128]{3,2,1,0:T(8,128)(2,1)S(1)}, f32[4,1,512]{2,1,0:T(1,128)S(1)}, f32[4,1,512]{2,1,0:T(1,128)S(1)}...) custom-call(s32[2]{0:T(128)S(1)} %pad_add_fusion.core_ref, ...), custom_call_target="tpu_custom_call" | custom-call | flops 6400000000 | bytes 1048576 | tf_op jit(solution)/shard_map/forward/pallas_call | solution.py:527
  53.4 0.2 collective-permute-start.2
  53.7 1.4 %collective-permute-done.2 = bf16[16,64,128]{2,1,0:T(8,128)(2,1)S(1)} collective-permute-done((bf16[16,64,128]{2,1,0:T(8,128)(2,1)S(1)}, bf16[16,64,128]{2,1,0:T(8,128)(2,1)S(1)}, u32[]{:S(2)}, u32[]{:S(2)}) %collective-permute-start.2) | collective-permute-done | bytes 262176 | tf_op jit(solution)/shard_map/ppermute | solution.py:548
  55.1 0.1 add_convert_fusion.after_ref
  55.1 2.0 %collective-permute-start.7 = (bf16[16,64,128]{2,1,0:T(8,128)(2,1)S(1)}, bf16[16,64,128]{2,1,0:T(8,128)(2,1)S(1)}, u32[]{:S(2)}, u32[]{:S(2)}) collective-permute-start(bf16[16,64,128]{2,1,0:T(8,128)(2,1)S(1)} %add_convert_fusion.after_ref), channel_id=1, source_target_pairs={{16,0},{32,16},{48,32},{64,48},{80,64},{96,80},{112,96},{128,112},... | collective-permute-start | bytes 786440 | tf_op jit(solution)/shard_map/ppermute | solution.py:550
  57.2 11.4 %own.1 = (bf16[16,384,128]{2,1,0:T(8,128)(2,1)S(1)}, bf16[16,128,128]{2,1,0:T(8,128)(2,1)S(1)}, bf16[8,64,128]{2,1,0:T(8,128)(2,1)S(1)}, bf16[8,64,128]{2,1,0:T(...) custom-call(s32[2]{0:T(128)S(1)} %pad_add_fusion.core_ref, ...), custom_call_target="tpu_custom_call", output_to_operand_aliasing={{0}: (8, {})} | custom-call | flops 4400000000 | bytes 1048576 | tf_op jit(solution)/shard_map/own/pallas_call | solution.py:551
  68.6 0.1 collective-permute-start.3
  68.8 0.5 collective-permute-start.4
  69.2 0.1 collective-permute-start.5
  69.3 0.4 collective-permute-start.6
  69.7 0.3 collective-permute-done.3.rest_0_
  70.1 0.2 collective-permute-done.4.rest_1_
  70.2 0.3 collective-permute-done.5.rest_2_
  70.6 0.2 collective-permute-done.6.rest_3_
  70.8 0.1 merge.1
  70.9 8.1 %collective-permute-done.7.back_ref = bf16[16,64,128]{2,1,0:T(8,128)(2,1)S(1)} collective-permute-done((bf16[16,64,128]{2,1,0:T(8,128)(2,1)S(1)}, bf16[16,64,128]{2,1,0:T(8,128)(2,1)S(1)}, u32[]{:S(2)}, u32[]{:S(2)}) %collective-permute-start.7) | collective-permute-done | bytes 262176 | tf_op jit(solution)/shard_map/ppermute | solution.py:550
  79.0 0.1 merge_back.1
  79.1 24.7 %all_to_all.11.t_ref = bf16[16,384,128]{2,1,0:T(8,128)(2,1)S(1)} all-to-all(bf16[16,384,128]{2,1,0:T(8,128)(2,1)S(1)} %merge_back.1), channel_id=1, replica_groups=mesh['dp'=16,'ctx'=16] {'ctx'}, dimensions={0} | all-to-all | bytes 3145728 | tf_op jit(solution)/shard_map/all_to_all | solution.py:595
  103.8 1.3 %unpack.1 = (bf16[128,2048]{1,0:T(8,128)(2,1)}, bf16[128,2048]{1,0:T(8,128)(2,1)}, bf16[128,512]{1,0:T(8,128)(2,1)}, bf16[128,512]{1,0:T(8,128)(2,1)}) custom-call(bf16[16,384,128]{2,1,0:T(8,128)(2,1)S(1)} %all_to_all.11.t_ref), custom_call_target="tpu_custom_call" | custom-call | flops 800000000 | bytes 1048576 | tf_op jit(solution)/shard_map/unpack/pallas_call | solution.py:596
  (5 shorter events, 0.1 us)
Async XLA Ops:
  1.5 11.8 %collective-permute-start = (bf16[128,512]{1,0:T(8,128)(2,1)S(1)}, bf16[128,512]{1,0:T(8,128)(2,1)S(1)}, u32[]{:S(2)}, u32[]{:S(2)}) collective-permute-start(bf16[128,512]{1,0:T(8,128)(2,1)S(1)} %pad_maximum_fusion), channel_id=1, source_target_pairs={{0,16},{16,32},{32,48},{48,64},{64,80},{80,96},{96,112},{112,128},... | collective-permute-start | bytes 393224 | tf_op jit(solution)/shard_map/ppermute | solution.py:500
  43.6 2.4 %collective-permute-start.1 = (bf16[16,192,128]{2,1,0:T(8,128)(2,1)S(1)}, bf16[16,192,128]{2,1,0:T(8,128)(2,1)S(1)}, u32[]{:S(2)}, u32[]{:S(2)}) collective-permute-start(bf16[16,192,128]{2,1,0:T(8,128)(2,1)S(1)} %slice.20), channel_id=1, source_target_pairs={{0,1},{1,0},{2,3},{3,2},{4,5},{5,4},{6,7},{7,6},{8,9},{9,8},{10,11... | collective-permute-start | bytes 2359304 | tf_op jit(solution)/shard_map/ppermute | solution.py:526
  53.4 1.6 %collective-permute-start.2 = (bf16[16,64,128]{2,1,0:T(8,128)(2,1)S(1)}, bf16[16,64,128]{2,1,0:T(8,128)(2,1)S(1)}, u32[]{:S(2)}, u32[]{:S(2)}) collective-permute-start(bf16[16,64,128]{2,1,0:T(8,128)(2,1)S(1)} %get-tuple-element.33), channel_id=1, source_target_pairs={{0,1},{1,0},{2,3},{3,2},{4,5},{5,4},{6,7},{7,6},{8,9},{9,8},{10,11... | collective-permute-start | bytes 786440 | tf_op jit(solution)/shard_map/ppermute | solution.py:548
  55.1 23.8 %collective-permute-start.7 = (bf16[16,64,128]{2,1,0:T(8,128)(2,1)S(1)}, bf16[16,64,128]{2,1,0:T(8,128)(2,1)S(1)}, u32[]{:S(2)}, u32[]{:S(2)}) collective-permute-start(bf16[16,64,128]{2,1,0:T(8,128)(2,1)S(1)} %add_convert_fusion.after_ref), channel_id=1, source_target_pairs={{16,0},{32,16},{48,32},{64,48},{80,64},{96,80},{112,96},{128,112},... | collective-permute-start | bytes 786440 | tf_op jit(solution)/shard_map/ppermute | solution.py:550
  68.6 1.4 %collective-permute-start.3 = (bf16[8,64,128]{2,1,0:T(8,128)(2,1)S(1)}, bf16[8,64,128]{2,1,0:T(8,128)(2,1)S(1)}, u32[]{:S(2)}, u32[]{:S(2)}) collective-permute-start(bf16[8,64,128]{2,1,0:T(8,128)(2,1)S(1)} %get-tuple-element.36), channel_id=1, source_target_pairs={{0,1},{1,0},{2,3},{3,2},{4,5},{5,4},{6,7},{7,6},{8,9},{9,8},{10,11... | collective-permute-start | bytes 393224 | tf_op jit(solution)/shard_map/ppermute | solution.py:574
  68.8 1.5 %collective-permute-start.4 = (bf16[8,64,128]{2,1,0:T(8,128)(2,1)S(1)}, bf16[8,64,128]{2,1,0:T(8,128)(2,1)S(1)}, u32[]{:S(2)}, u32[]{:S(2)}) collective-permute-start(bf16[8,64,128]{2,1,0:T(8,128)(2,1)S(1)} %get-tuple-element.37), channel_id=1, source_target_pairs={{0,1},{1,0},{2,3},{3,2},{4,5},{5,4},{6,7},{7,6},{8,9},{9,8},{10,11... | collective-permute-start | bytes 393224 | tf_op jit(solution)/shard_map/ppermute | solution.py:574
  69.2 1.3 %collective-permute-start.5 = (bf16[8,64,128]{2,1,0:T(8,128)(2,1)S(1)}, bf16[8,64,128]{2,1,0:T(8,128)(2,1)S(1)}, u32[]{:S(2)}, u32[]{:S(2)}) collective-permute-start(bf16[8,64,128]{2,1,0:T(8,128)(2,1)S(1)} %get-tuple-element.38), channel_id=1, source_target_pairs={{0,1},{1,0},{2,3},{3,2},{4,5},{5,4},{6,7},{7,6},{8,9},{9,8},{10,11... | collective-permute-start | bytes 393224 | tf_op jit(solution)/shard_map/ppermute | solution.py:574
  69.3 1.4 %collective-permute-start.6 = (bf16[8,64,128]{2,1,0:T(8,128)(2,1)S(1)}, bf16[8,64,128]{2,1,0:T(8,128)(2,1)S(1)}, u32[]{:S(2)}, u32[]{:S(2)}) collective-permute-start(bf16[8,64,128]{2,1,0:T(8,128)(2,1)S(1)} %get-tuple-element.39), channel_id=1, source_target_pairs={{0,1},{1,0},{2,3},{3,2},{4,5},{5,4},{6,7},{7,6},{8,9},{9,8},{10,11... | collective-permute-start | bytes 393224 | tf_op jit(solution)/shard_map/ppermute | solution.py:574
